TPU v7x, 32 devices: a whole 2x2x4 slice. The times are simulated.
32 devices in a mesh: sec: 2 (over core), section: 4 (over z), expert: 4 (over y, x).
Axes of the slice: x: 2, y: 2, z: 4, core: 2. Of those that a mesh axis runs over, the one named last changes fastest.
Arguments:
- tokens: bfloat16 [512, 2048], P('expert', ('sec', 'section')), may hold values from -6 to 6
- cotangent: bfloat16 [512, 2048], P('expert', ('sec', 'section')), may hold values from -6 to 6
- expert_ids: int32 [512, 2], P('expert'), may hold values from 0 to 3, all different within a row; in each aligned block of 128 rows (0 to 127, 128 to 255, ...) at most 96 rows name the same one
- gate_values: float32 [512, 2], P('expert'), may hold values from 0.2 to 1
- expand_weight: bfloat16 [4, 2048, 4096], P('expert', None, ('sec', 'section')), may hold values from -0.125 to 0.125
- contract_weight: bfloat16 [4, 4096, 2048], P('expert', ('sec', 'section')), may hold values from -0.09375 to 0.09375
Outputs:
- combined: bfloat16 [512, 2048], P('expert', ('sec', 'section'))
- input_grad: bfloat16 [512, 2048], P('expert', ('sec', 'section'))
- gate_grad: float32 [512, 2], P('expert')
Inputs may be any that keep to these rules, and one draw needn't show every extreme that they name: `expert_ids`: the two ids of a token differ. Among the 128 tokens of one index of expert, no expert is named by more than 96 of them, a bound that some block reaches.
All inputs are finite; a program needn't handle non-finite values.
Results may differ from a plain program's by a relative error of at most 0.015.
Values may be sent and summed in bfloat16 or wider, within the bound.
A program may use at most 64 MiB of HBM per device.

v0:
```python
import math

import jax
import jax.numpy as jnp
from jax import lax
from jax.sharding import PartitionSpec as P

gelu_coef = math.sqrt(2.0 / math.pi)
gelu_cubic = 0.044715


def gelu_parts(hidden):
    inner_arg = gelu_coef * (hidden + gelu_cubic * hidden * hidden * hidden)
    tanh_value = jnp.tanh(inner_arg)
    activation = 0.5 * hidden * (1.0 + tanh_value)
    derivative = 0.5 * (1.0 + tanh_value) + 0.5 * hidden * (
        1.0 - tanh_value * tanh_value
    ) * gelu_coef * (1.0 + 3.0 * gelu_cubic * hidden * hidden)
    return (activation, derivative)


def slot_positions(expert_ids, capacity, experts):
    flat_ids = expert_ids.reshape(-1)
    one_hot = (flat_ids[:, None] == jnp.arange(experts, dtype=jnp.int32)[None, :]).astype(jnp.int32)
    earlier = jnp.sum((jnp.cumsum(one_hot, axis=0) - one_hot) * one_hot, axis=1)
    return flat_ids * capacity + earlier


def transposed_product(left, right):
    return lax.dot_general(
        left, right, (((1,), (1,)), ((), ())), preferred_element_type=jnp.float32
    )


def per_device(tokens, cotangent, expert_ids, gate_values, expand_weight, contract_weight):
    block_index = lax.axis_index("sec") * lax.axis_size("section") + lax.axis_index("section")
    tok_rows, width_share = tokens.shape
    experts = lax.axis_size("expert")
    capacity = 3 * tok_rows // experts
    slot_count = experts * capacity
    expand_local = expand_weight[0]
    contract_local = contract_weight[0]
    full_width = contract_local.shape[1]
    positions = slot_positions(expert_ids, capacity, experts)
    placement_matrix = (
        positions[:, None] == jnp.arange(slot_count, dtype=jnp.int32)[None, :]
    ).astype(jnp.bfloat16)
    scaled_grad = (gate_values[:, :, None] * cotangent[:, None, :].astype(jnp.float32)).astype(
        jnp.bfloat16
    )

    def to_slots(pairs):
        return jnp.dot(placement_matrix.T, pairs, preferred_element_type=jnp.float32).astype(
            jnp.bfloat16
        )

    whole_tokens, whole_grad = (
        lax.all_gather(tokens, ("sec", "section"), axis=1, tiled=True),
        lax.all_gather(scaled_grad, ("sec", "section"), axis=2, tiled=True),
    )
    pair_tokens = jnp.broadcast_to(whole_tokens[:, None, :], (tok_rows, 2, full_width)).reshape(
        2 * tok_rows, full_width
    )
    send_x = to_slots(pair_tokens).reshape(experts, capacity, full_width)
    send_g = to_slots(whole_grad.reshape(2 * tok_rows, full_width)).reshape(
        experts, capacity, full_width
    )
    recv_x, recv_g = (
        lax.all_to_all(send_x, "expert", split_axis=0, concat_axis=0, tiled=True),
        lax.all_to_all(send_g, "expert", split_axis=0, concat_axis=0, tiled=True),
    )
    hidden = jnp.dot(
        recv_x.reshape(slot_count, full_width), expand_local, preferred_element_type=jnp.float32
    )
    grad_activation = transposed_product(recv_g.reshape(slot_count, full_width), contract_local)
    activation, derivative = gelu_parts(hidden)
    activation = activation.astype(jnp.bfloat16)
    grad_hidden = (grad_activation * derivative).astype(jnp.bfloat16)
    out_part = jnp.dot(activation, contract_local, preferred_element_type=jnp.float32).astype(
        jnp.bfloat16
    )
    back_part = transposed_product(grad_hidden, expand_local).astype(jnp.bfloat16)
    out_sum, back_sum = (
        lax.psum(out_part, ("sec", "section")).astype(jnp.float32),
        lax.psum(back_part, ("sec", "section")).astype(jnp.float32),
    )
    out_rows = out_sum.astype(jnp.bfloat16).reshape(experts, capacity, full_width)
    back_rows = back_sum.astype(jnp.bfloat16).reshape(experts, capacity, full_width)
    returned_out, returned_back = (
        lax.all_to_all(out_rows, "expert", split_axis=0, concat_axis=0, tiled=True),
        lax.all_to_all(back_rows, "expert", split_axis=0, concat_axis=0, tiled=True),
    )
    returned_out = lax.dynamic_slice_in_dim(returned_out, block_index * width_share, width_share, 2)
    returned_back = lax.dynamic_slice_in_dim(
        returned_back, block_index * width_share, width_share, 2
    )
    out_pairs = jnp.dot(
        placement_matrix,
        returned_out.reshape(slot_count, width_share),
        preferred_element_type=jnp.float32,
    ).reshape(tok_rows, 2, width_share)
    back_pairs = jnp.dot(
        placement_matrix,
        returned_back.reshape(slot_count, width_share),
        preferred_element_type=jnp.float32,
    ).reshape(tok_rows, 2, width_share)
    combined = jnp.sum(gate_values[:, :, None] * out_pairs, axis=1).astype(jnp.bfloat16)
    partial_dots = jnp.sum(cotangent[:, None, :].astype(jnp.float32) * out_pairs, axis=2)
    gate_grad = lax.psum(partial_dots, ("sec", "section"))
    input_grad = (back_pairs[:, 0, :] + back_pairs[:, 1, :]).astype(jnp.bfloat16)
    return (combined, input_grad, gate_grad)


def solution(mesh):
    return jax.shard_map(
        per_device,
        mesh=mesh,
        in_specs=(
            P("expert", ("sec", "section")),
            P("expert", ("sec", "section")),
            P("expert", None),
            P("expert", None),
            P("expert", None, ("sec", "section")),
            P("expert", ("sec", "section"), None),
        ),
        out_specs=(
            P("expert", ("sec", "section")),
            P("expert", ("sec", "section")),
            P("expert", None),
        ),
        check_vma=False,
    )
```

profile of v0, /device:TPU:0, one launch (start us, length us, event | category | flops | bytes accessed | tf_op | source)
XLA Modules:
  0.0 251.3 jit_solution(7560205527923228213)
XLA Ops:
  7.2 1.0 convert_element_type.53
  8.2 1.4 multiply_convert_fusion.2
  10.6 30.0 %all_gather.6 = bf16[128,2048]{1,0:T(8,128)(2,1)S(1)} all-gather(bf16[128,256]{1,0:T(8,128)(2,1)} %param.6), channel_id=1, replica_groups=mesh['sec'=2,'section'=4,'expert'=4] {'sec','section'}, dimensions={1}, use_global_device_ids=true | all-gather | bytes 589824 | tf_op jit(solution)/shard_map/all_gather | solution.py:58
  40.8 1.2 reduce-window.6
  42.3 1.6 broadcast_in_dim.2
  43.9 1.5 reshape.109
  45.5 1.8 convolution_convert_fusion.3
  47.4 4.3 %all-to-all-start = ((bf16[4,96,2048]{2,1,0:T(8,128)(2,1)}), bf16[4,96,2048]{2,1,0:T(8,128)(2,1)}, u32[]{:S(2)}, u32[]{:S(2)}) async-start(bf16[4,96,2048]{2,1,0:T(8,128)(2,1)} %bitcast.61), calls=%async_computation | async-start | bytes 3145728 | tf_op jit(solution)/shard_map/all_to_all | solution.py:69
  51.7 3.3 %copy.24 = bf16[128,2,2048]{2,1,0:T(2,128)(2,1)} copy(bf16[128,2,2048]{2,0,1:T(8,128)(2,1)} %all-gather.2.cloned.1.call-done) | data formatting | bytes 2097152 | tf_op jit(solution)/shard_map/all_gather | solution.py:59
  55.0 1.5 reshape.114
  56.5 1.9 convolution_convert_fusion.1
  58.3 14.0 %all-to-all-done = bf16[4,96,2048]{2,1,0:T(8,128)(2,1)} async-done(((bf16[4,96,2048]{2,1,0:T(8,128)(2,1)}), bf16[4,96,2048]{2,1,0:T(8,128)(2,1)}, u32[]{:S(2)}, u32[]{:S(2)}) %all-to-all-start) | async-done | bytes 1572896 | tf_op jit(solution)/shard_map/all_to_all | solution.py:69
  72.4 4.3 %all-to-all-start.2 = ((bf16[4,96,2048]{2,1,0:T(8,128)(2,1)}), bf16[4,96,2048]{2,1,0:T(8,128)(2,1)}, u32[]{:S(2)}, u32[]{:S(2)}) async-start(bf16[4,96,2048]{2,1,0:T(8,128)(2,1)} %bitcast.62), calls=%async_computation.2 | async-start | bytes 3145728 | tf_op jit(solution)/shard_map/all_to_all | solution.py:70
  76.8 3.0 %fusion.4 = f32[384,512]{1,0:T(8,128)S(1)} fusion(bf16[384,2048]{1,0:T(8,128)(2,1)} %bitcast.4, bf16[1,2048,512]{2,1,0:T(8,128)(2,1)} %param.10), kind=kOutput, calls=%fused_computation.8 | convolution fusion | flops 805306368 | bytes 4456448 | tf_op jit(solution)/shard_map/dot_general | solution.py:72
  79.8 2.2 convolution_convert_fusion.2
  82.0 14.6 %all-to-all-done.2 = bf16[4,96,2048]{2,1,0:T(8,128)(2,1)} async-done(((bf16[4,96,2048]{2,1,0:T(8,128)(2,1)}), bf16[4,96,2048]{2,1,0:T(8,128)(2,1)}, u32[]{:S(2)}, u32[]{:S(2)}) %all-to-all-start.2) | async-done | bytes 1572896 | tf_op jit(solution)/shard_map/all_to_all | solution.py:70
  96.6 5.4 %convolution_convert_fusion = bf16[384,2048]{1,0:T(8,128)(2,1)} fusion(bf16[1,2048,512]{2,1,0:T(8,128)(2,1)} %param.10, bf16[384,2048]{1,0:T(8,128)(2,1)} %bitcast.11, bf16[1,512,2048]{2,1,0:T(8,128)(2,1)S(1)} %copy-done, f32[384,512]{1,0:T(8,128)S(1)} %fusion.4), kind=kOutput, calls=%fused_computation | convolution fusion | flops 1615134720 | bytes 8126464 | tf_op jit(solution)/shard_map/dot_general | solution.py:30
  102.0 76.7 %all-reduce.3.cloned.1.call-done = (bf16[4,96,2048]{2,1,0:T(8,128)(2,1)}, bf16[4,96,2048]{2,1,0:T(8,128)(2,1)}) async-done(((bf16[4,96,2048]{2,1,0:T(8,128)(2,1)}, bf16[4,96,2048]{2,1,0:T(8,128)(2,1)}), (bf16[4,96,2048]{2,1,0:T(8,128)(2,1)}, bf16[4,96,2048]{2,1,0:T(8,128)(2,1)})) %all-reduce.3.cloned.1.call-update) | async-done | bytes 3145744 | tf_op jit(solution)/shard_map/psum | solution.py:84
  178.8 24.0 %all_to_all.20 = bf16[4,96,2048]{2,1,0:T(8,128)(2,1)} all-to-all(bf16[4,96,2048]{2,1,0:T(8,128)(2,1)} %get-tuple-element.5), channel_id=1, replica_groups=mesh['sec'=2,'section'=4,'expert'=4] {'expert'}, dimensions={0} | all-to-all | bytes 3145728 | tf_op jit(solution)/shard_map/all_to_all | solution.py:90
  202.8 4.5 %all-to-all-start.3 = ((bf16[4,96,2048]{2,1,0:T(8,128)(2,1)}), bf16[4,96,2048]{2,1,0:T(8,128)(2,1)}, u32[]{:S(2)}, u32[]{:S(2)}) async-start(bf16[4,96,2048]{2,1,0:T(8,128)(2,1)} %get-tuple-element.6), calls=%async_computation.3 | async-start | bytes 3145728 | tf_op jit(solution)/shard_map/all_to_all | solution.py:91
  207.5 17.6 %all-to-all-done.3 = bf16[4,96,2048]{2,1,0:T(8,128)(2,1)} async-done(((bf16[4,96,2048]{2,1,0:T(8,128)(2,1)}), bf16[4,96,2048]{2,1,0:T(8,128)(2,1)}, u32[]{:S(2)}, u32[]{:S(2)}) %all-to-all-start.3) | async-done | bytes 1572896 | tf_op jit(solution)/shard_map/all_to_all | solution.py:91
  225.1 1.1 constant_dynamic-slice_fusion
  227.1 1.0 multiply_reduce_fusion
  228.1 16.4 %psum.23 = f32[128,2]{0,1:T(2,128)} all-reduce(f32[128,2]{0,1:T(2,128)S(1)} %get-tuple-element.3), channel_id=1, replica_groups=mesh['sec'=2,'section'=4,'expert'=4] {'sec','section'}, use_global_device_ids=true, to_apply=%region_7.8 | all-reduce | flops 256 | bytes 2048 | tf_op jit(solution)/shard_map/psum | solution.py:109
  (28 shorter events, 2.8 us)
Async XLA Ops:
  7.2 72.7 %copy-start = (bf16[1,512,2048]{2,1,0:T(8,128)(2,1)S(1)}, bf16[1,512,2048]{2,1,0:T(8,128)(2,1)}, u32[]{:S(2)}) copy-start(bf16[1,512,2048]{2,1,0:T(8,128)(2,1)} %param.11) | copy-start | bytes 6291460
  7.2 44.5 %all-gather.2.cloned.1.call-start = ((), (), s32[]{:S(2)}) async-start(), calls=%async_computation.4 | async-start | bytes 1179648 | tf_op jit(solution)/shard_map/all_gather | solution.py:59
  47.4 25.0 %all-to-all-start = ((bf16[4,96,2048]{2,1,0:T(8,128)(2,1)}), bf16[4,96,2048]{2,1,0:T(8,128)(2,1)}, u32[]{:S(2)}, u32[]{:S(2)}) async-start(bf16[4,96,2048]{2,1,0:T(8,128)(2,1)} %bitcast.61), calls=%async_computation | async-start | bytes 3145728 | tf_op jit(solution)/shard_map/all_to_all | solution.py:69
  72.4 24.2 %all-to-all-start.2 = ((bf16[4,96,2048]{2,1,0:T(8,128)(2,1)}), bf16[4,96,2048]{2,1,0:T(8,128)(2,1)}, u32[]{:S(2)}, u32[]{:S(2)}) async-start(bf16[4,96,2048]{2,1,0:T(8,128)(2,1)} %bitcast.62), calls=%async_computation.2 | async-start | bytes 3145728 | tf_op jit(solution)/shard_map/all_to_all | solution.py:70
  76.7 102.1 %all-reduce.3.cloned.1.call-start = ((), (), s32[]{:S(2)}) async-start(), calls=%async_computation.5 | async-start | bytes 6291456 | tf_op jit(solution)/shard_map/psum | solution.py:84
  202.8 4.7 %copy-start.1 = (s32[128,2]{0,1:T(2,128)S(1)}, s32[128,2]{0,1:T(2,128)}, u32[]{:S(2)}) copy-start(s32[128,2]{0,1:T(2,128)} %param.8) | copy-start | bytes 3076
  202.8 22.3 %all-to-all-start.3 = ((bf16[4,96,2048]{2,1,0:T(8,128)(2,1)}), bf16[4,96,2048]{2,1,0:T(8,128)(2,1)}, u32[]{:S(2)}, u32[]{:S(2)}) async-start(bf16[4,96,2048]{2,1,0:T(8,128)(2,1)} %get-tuple-element.6), calls=%async_computation.3 | async-start | bytes 3145728 | tf_op jit(solution)/shard_map/all_to_all | solution.py:91
  207.2 19.8 %copy-start.2 = (f32[128,2]{0,1:T(2,128)S(1)}, f32[128,2]{0,1:T(2,128)}, u32[]{:S(2)}) copy-start(f32[128,2]{0,1:T(2,128)} %param.9) | copy-start | bytes 3076
Sparse Core Ops, SparseCore 0:
  9.8 30.5 all-gather.1
  102.2 76.5 all-reduce.2
where the time goes:
time: 253 us; the launch traced here: 251 us
  waiting for transfers between devices  123 us (49%)
  blocking collectives  70.4 us (28%)
  matrix products  15.7 us (6%)
  between operations  14.2 us (6%)
  starting transfers between devices  13.2 us (5%)
  local copies, waits for them, and re-layouts  10.4 us (4%)
  other arithmetic  4.44 us (2%)
    psum x1, waiting for transfers between devices, per_device(): lax.psum(out_part, ('sec', 'section')).astype(jnp.float32)  76.7 us
    all_gather x1, blocking collectives, per_device(): lax.all_gather(tokens, ('sec', 'section'), axis=1, tiled=True)  30 us
    all_to_all x1, blocking collectives, per_device(): lax.all_to_all(out_rows, 'expert', split_axis=0, concat_axis=0, tiled=True)  24 us
    all_to_all x1, waiting for transfers between devices, per_device(): lax.all_to_all(back_rows, 'expert', split_axis=0, concat_axis=0, tiled=True)  17.6 us
    psum x1, blocking collectives, per_device(): gate_grad = lax.psum(partial_dots, ('sec', 'section'))  16.4 us
    all_to_all x1, waiting for transfers between devices, per_device(): lax.all_to_all(send_g, 'expert', split_axis=0, concat_axis=0, tiled=True)  14.6 us
    all_to_all x1, waiting for transfers between devices, per_device(): lax.all_to_all(send_x, 'expert', split_axis=0, concat_axis=0, tiled=True)  14 us
    dot_general x1, matrix products, transposed_product(): lax.dot_general(left, right, (((1,), (1,)), ((), ())), preferred_element_...  5.43 us
  transfers between devices with their start and end apart: 5, of which 4 were waited for; matrix products, arithmetic and copies ran while one was open for 8% of the time, Pallas kernels for 0%

commit v1 on v0

--- a/solution.py
+++ b/solution.py
@@ -3,7 +3,338 @@
 import jax
 import jax.numpy as jnp
 from jax import lax
+from jax.experimental import pallas as pl
+from jax.experimental.pallas import tpu as pltpu
 from jax.sharding import PartitionSpec as P
+
+MESH = pl.DeviceIdType.MESH
+F32 = jnp.float32
+BF16 = jnp.bfloat16
+
+
+def partners(i):
+    return (i, i + 1 - 2 * lax.rem(i, 2), lax.rem(i + 2, 4), 3 - i)
+
+
+def kernel(
+    tok, cot, ids, gate, w1_hbm, w2_hbm,
+    comb_out, grad_out, gg_out,
+    w1, w2, zbuf, sendbuf, slots, pt, gslot, pmat, pgate, hid, gact, act, ghid,
+    own, sibs, sibr, rsend, ret, xsend, xret, gbuf, zs2, zr2, keep,
+    wsem, zsend, zrecv, asend, arecv, fsend, frecv, bsend, brecv,
+    rs_send, rs_recv, x_send, x_recv, g_send, g_recv, q_send, q_recv,
+):
+    cap = slots.shape[4]
+    wd = slots.shape[5]
+    tr = tok.shape[0]
+    rows = 4 * cap
+    c = lax.axis_index("sec")
+    z = lax.axis_index("section")
+    e = lax.axis_index("expert")
+    zp = partners(z)
+    ep = partners(e)
+
+    def to_z(s):
+        return {"section": zp[s]}
+
+    def to_e(d):
+        return {"expert": ep[d]}
+
+    sib = {"sec": 1 - c}
+
+    def rcopy(src, dst, ss, rs, dev):
+        return pltpu.make_async_remote_copy(
+            src_ref=src, dst_ref=dst, send_sem=ss, recv_sem=rs,
+            device_id=dev, device_id_type=MESH,
+        )
+
+    cw1 = pltpu.make_async_copy(w1_hbm.at[0], w1, wsem.at[0])
+    cw2 = pltpu.make_async_copy(w2_hbm.at[0], w2, wsem.at[1])
+    cw1.start()
+    cw2.start()
+
+    zbuf[0, 0] = tok[...]
+    zbuf[0, 1] = cot[...]
+    barrier = pltpu.get_barrier_semaphore()
+    peers = [to_z(s) for s in (1, 2, 3)] + [to_e(d) for d in (1, 2, 3)] + [sib]
+    peers += [{"section": zp[s], "sec": 1 - c} for s in (1, 2, 3)]
+    for p in peers:
+        pl.semaphore_signal(barrier, inc=1, device_id=p, device_id_type=MESH)
+    pl.semaphore_wait(barrier, len(peers))
+
+    sends = []
+    zc = {}
+    for s in (1, 2, 3):
+        zc[s] = rcopy(zbuf.at[0], zbuf.at[s], zsend.at[s], zrecv.at[s], to_z(s))
+        zc[s].start()
+        sends.append(zc[s])
+
+    rid = lax.broadcasted_iota(jnp.int32, (8, tr), 0)
+    erow = jnp.where(rid == 0, ep[0], jnp.where(rid == 1, ep[1], jnp.where(rid == 2, ep[2], jnp.where(rid == 3, ep[3], -1))))
+    is0 = ids[0:1, :] == erow
+    is1 = ids[1:2, :] == erow
+    named = jnp.where(is0, 1.0, jnp.where(is1, 1.0, 0.0)).astype(F32)
+    gates = jnp.where(is0, gate[0:1, :], jnp.where(is1, gate[1:2, :], 0.0))
+    upper = (
+        lax.broadcasted_iota(jnp.int32, (tr, tr), 0) < lax.broadcasted_iota(jnp.int32, (tr, tr), 1)
+    ).astype(F32).astype(BF16)
+    rank = jnp.dot(named.astype(BF16), upper, preferred_element_type=F32)
+    key = jnp.where(named > 0.5, rank, -1.0).astype(jnp.int32)
+    cid = lax.broadcasted_iota(jnp.int32, (cap, tr), 0)
+    for d in range(4):
+        hit = cid == key[d : d + 1, :]
+        one = jnp.where(hit, 1.0, 0.0).astype(F32)
+        weighed = jnp.where(hit, gates[d : d + 1, :], 0.0)
+        pt[d] = one.astype(BF16)
+        gslot[d] = jnp.broadcast_to(jnp.sum(weighed, axis=1, keepdims=True), (cap, wd))
+        own[0, 0, d * cap : (d + 1) * cap, 0:tr] = one
+        own[0, 1, d * cap : (d + 1) * cap, 0:tr] = weighed
+    pmat[...] = own[0, 0, :, 0:tr].T.astype(BF16)
+    pgate[...] = own[0, 1, :, 0:tr].T.astype(BF16)
+
+    cw1.wait()
+    cw2.wait()
+
+    def block(core, s):
+        return pl.ds(pl.multiple_of((core * 4 + zp[s]) * wd, wd), wd)
+
+    def gather_step(half, core, s, first):
+        at = block(core, s)
+        xs = slots[half, s, :, 0].reshape(rows, wd)
+        gs = slots[half, s, :, 1].reshape(rows, wd)
+        hpart = jnp.dot(xs, w1[at, :], preferred_element_type=F32)
+        gpart = lax.dot_general(gs, w2[:, at], (((1,), (1,)), ((), ())), preferred_element_type=F32)
+        if first:
+            hid[...] = hpart
+            gact[...] = gpart
+        else:
+            hid[...] += hpart
+            gact[...] += gpart
+
+    ac = {}
+    fc = {}
+
+    def dispatch(s):
+        if s:
+            zc[s].wait_recv()
+        xb = zbuf[s, 0]
+        cb = zbuf[s, 1]
+        for d in (3, 1, 2, 0):
+            dst = slots.at[0, s, 0] if d == 0 else sendbuf.at[s, d]
+            dst[0] = jnp.dot(pt[d], xb, preferred_element_type=F32).astype(BF16)
+            dst[1] = (jnp.dot(pt[d], cb, preferred_element_type=F32) * gslot[d]).astype(BF16)
+            if d:
+                ac[s, d] = rcopy(sendbuf.at[s, d], slots.at[0, s, d], asend.at[s, d], arecv.at[s, d], to_e(d))
+                ac[s, d].start()
+                sends.append(ac[s, d])
+
+    def take(s):
+        for d in (1, 2, 3):
+            ac[s, d].wait_recv()
+        fc[s] = rcopy(slots.at[0, s], slots.at[1, s], fsend.at[s], frecv.at[s], sib)
+        fc[s].start()
+        sends.append(fc[s])
+        gather_step(0, c, s, s == 0)
+
+    def take_sib(s):
+        fc[s].wait_recv()
+        gather_step(1, 1 - c, s, False)
+
+    dispatch(0)
+    dispatch(1)
+    take(0)
+    dispatch(2)
+    take(1)
+    take_sib(0)
+    dispatch(3)
+    take(2)
+    take_sib(1)
+    take(3)
+    take_sib(2)
+    take_sib(3)
+
+    coef = math.sqrt(2.0 / math.pi)
+    cubic = 0.044715
+    lane = lax.broadcasted_iota(jnp.int32, (cap, 128), 1)
+    xc = {}
+    for d in (3, 1, 2, 0):
+        rr = slice(d * cap, (d + 1) * cap)
+        h = hid[rr, :]
+        ga = gact[rr, :]
+        h2 = h * h
+        u = jnp.tanh(coef * h * (1.0 + cubic * h2))
+        half = 0.5 * (1.0 + u)
+        a = (h * half).astype(BF16)
+        act[rr, :] = a
+        ghid[rr, :] = (ga * (half + 0.5 * h * (1.0 - u * u) * coef * (1.0 + 3.0 * cubic * h2))).astype(BF16)
+        dots = jnp.sum(a.astype(F32) * ga, axis=1, keepdims=True)
+        hi = dots.astype(BF16).astype(F32)
+        lo = dots - hi
+        extra = jnp.where(lane == 2 * d, hi, jnp.where(lane == 2 * d + 1, lo, 0.0)).astype(BF16)
+        if d:
+            xsend[d] = extra
+            xc[d] = rcopy(xsend.at[d], xret.at[d], x_send.at[d], x_recv.at[d], to_e(d))
+            xc[d].start()
+            sends.append(xc[d])
+        else:
+            xret[0] = extra
+
+    bc = {}
+    rc = {}
+    qc = {}
+
+    def expand_back(s):
+        for core, mine in ((1 - c, False), (c, True)):
+            at = block(core, s)
+            o = jnp.dot(act[...], w2[:, at], preferred_element_type=F32)
+            b = lax.dot_general(ghid[...], w1[at, :], (((1,), (1,)), ((), ())), preferred_element_type=F32)
+            if mine:
+                own[s, 0] = o
+                own[s, 1] = b
+            else:
+                sibs[s, 0] = o.astype(BF16)
+                sibs[s, 1] = b.astype(BF16)
+                bc[s] = rcopy(sibs.at[s], sibr.at[s], bsend.at[s], brecv.at[s], sib)
+                bc[s].start()
+                sends.append(bc[s])
+
+    def give_back(s):
+        bc[s].wait_recv()
+        for d in (3, 1, 2, 0):
+            rr = slice(d * cap, (d + 1) * cap)
+            dst = ret.at[s, 0] if d == 0 else rsend.at[s, d]
+            for k in range(2):
+                dst[k] = (own[s, k, rr, :] + sibr[s, k, rr, :].astype(F32)).astype(BF16)
+            if d:
+                rc[s, d] = rcopy(rsend.at[s, d], ret.at[s, d], rs_send.at[s, d], rs_recv.at[s, d], to_e(d))
+                rc[s, d].start()
+                sends.append(rc[s, d])
+
+    def join(s):
+        for d in (1, 2, 3):
+            rc[s, d].wait_recv()
+        o = jnp.dot(pgate[...], ret[s, :, 0].reshape(rows, wd), preferred_element_type=F32)
+        b = jnp.dot(pmat[...], ret[s, :, 1].reshape(rows, wd), preferred_element_type=F32)
+        if s:
+            zs2[s, 0] = o.astype(BF16)
+            zs2[s, 1] = b.astype(BF16)
+            qc[s] = rcopy(zs2.at[s], zr2.at[s], q_send.at[s], q_recv.at[s], to_z(s))
+            qc[s].start()
+            sends.append(qc[s])
+        else:
+            keep[0] = o
+            keep[1] = b
+
+    expand_back(3)
+    expand_back(2)
+    give_back(3)
+    expand_back(1)
+    give_back(2)
+    expand_back(0)
+    give_back(1)
+    give_back(0)
+
+    for d in (1, 2, 3):
+        xc[d].wait_recv()
+    share = jnp.dot(pmat[...], xret[...].reshape(rows, 128), preferred_element_type=F32)
+    gbuf[0] = share.T[0:8, :]
+    gc = []
+    for i, dev in enumerate([to_z(1), to_z(2), to_z(3), sib] + [{"section": zp[s], "sec": 1 - c} for s in (1, 2, 3)]):
+        g = rcopy(gbuf.at[0], gbuf.at[i + 1], g_send.at[i], g_recv.at[i], dev)
+        g.start()
+        sends.append(g)
+        gc.append(g)
+
+    join(3)
+    join(2)
+    join(1)
+    join(0)
+
+    for g in gc:
+        g.wait_recv()
+    total = gbuf[0]
+    for i in range(7):
+        total = total + gbuf[i + 1]
+    for k in range(2):
+        acc = jnp.zeros((1, tr), F32)
+        for d in range(4):
+            v = total[2 * d : 2 * d + 1, :] + total[2 * d + 1 : 2 * d + 2, :]
+            acc = acc + jnp.where(ids[k : k + 1, :] == ep[d], v, 0.0)
+        gg_out[k : k + 1, :] = acc / gate[k : k + 1, :]
+
+    for s in (1, 2, 3):
+        qc[s].wait_recv()
+    for k, out in ((0, comb_out), (1, grad_out)):
+        v = keep[k]
+        for s in (1, 2, 3):
+            v = v + zr2[s, k].astype(F32)
+        out[...] = v.astype(BF16)
+
+    for d in sends:
+        d.wait_send()
+
+
+def fused(tokens, cotangent, expert_ids, gate_values, expand_weight, contract_weight):
+    tr, wd = tokens.shape
+    cap = 3 * tr // 4
+    width, ff = expand_weight.shape[1:]
+    rows = 4 * cap
+    vm = pl.BlockSpec(memory_space=pltpu.VMEM)
+    anyspace = pl.BlockSpec(memory_space=pl.ANY)
+    dma = pltpu.SemaphoreType.DMA
+    comb, grad, gg = pl.pallas_call(
+        kernel,
+        out_shape=(
+            jax.ShapeDtypeStruct((tr, wd), BF16),
+            jax.ShapeDtypeStruct((tr, wd), BF16),
+            jax.ShapeDtypeStruct((2, tr), F32),
+        ),
+        in_specs=[vm, vm, vm, vm, anyspace, anyspace],
+        out_specs=(vm, vm, vm),
+        scratch_shapes=[
+            pltpu.VMEM((width, ff), BF16),
+            pltpu.VMEM((ff, width), BF16),
+            pltpu.VMEM((4, 2, tr, wd), BF16),
+            pltpu.VMEM((4, 4, 2, cap, wd), BF16),
+            pltpu.VMEM((2, 4, 4, 2, cap, wd), BF16),
+            pltpu.VMEM((4, cap, tr), BF16),
+            pltpu.VMEM((4, cap, wd), F32),
+            pltpu.VMEM((tr, rows), BF16),
+            pltpu.VMEM((tr, rows), BF16),
+            pltpu.VMEM((rows, ff), F32),
+            pltpu.VMEM((rows, ff), F32),
+            pltpu.VMEM((rows, ff), BF16),
+            pltpu.VMEM((rows, ff), BF16),
+            pltpu.VMEM((4, 2, rows, wd), F32),
+            pltpu.VMEM((4, 2, rows, wd), BF16),
+            pltpu.VMEM((4, 2, rows, wd), BF16),
+            pltpu.VMEM((4, 4, 2, cap, wd), BF16),
+            pltpu.VMEM((4, 4, 2, cap, wd), BF16),
+            pltpu.VMEM((4, cap, 128), BF16),
+            pltpu.VMEM((4, cap, 128), BF16),
+            pltpu.VMEM((8, 8, tr), F32),
+            pltpu.VMEM((4, 2, tr, wd), BF16),
+            pltpu.VMEM((4, 2, tr, wd), BF16),
+            pltpu.VMEM((2, tr, wd), F32),
+            dma((2,)),
+            dma((4,)), dma((4,)),
+            dma((4, 4)), dma((4, 4)),
+            dma((4,)), dma((4,)),
+            dma((4,)), dma((4,)),
+            dma((4, 4)), dma((4, 4)),
+            dma((4,)), dma((4,)),
+            dma((7,)), dma((7,)),
+            dma((4,)), dma((4,)),
+        ],
+        compiler_params=pltpu.CompilerParams(
+            collective_id=0, has_side_effects=True, vmem_limit_bytes=48 * 1024 * 1024
+        ),
+        cost_estimate=pl.CostEstimate(
+            flops=8 * rows * width * ff, bytes_accessed=4 * width * ff, transcendentals=rows * ff
+        ),
+    )(tokens, cotangent, expert_ids.T, gate_values.T, expand_weight, contract_weight)
+    return comb, grad, gg.T
+
 
 gelu_coef = math.sqrt(2.0 / math.pi)
 gelu_cubic = 0.044715
@@ -19,10 +350,11 @@
     return (activation, derivative)
 
 
-def slot_positions(expert_ids, capacity, experts):
+def slot_positions(expert_ids, capacity):
     flat_ids = expert_ids.reshape(-1)
-    one_hot = (flat_ids[:, None] == jnp.arange(experts, dtype=jnp.int32)[None, :]).astype(jnp.int32)
-    earlier = jnp.sum((jnp.cumsum(one_hot, axis=0) - one_hot) * one_hot, axis=1)
+    place = jnp.arange(flat_ids.shape[0], dtype=jnp.int32)
+    same = (flat_ids[:, None] == flat_ids[None, :]) & (place[None, :] < place[:, None])
+    earlier = jnp.sum(same.astype(jnp.int32), axis=1)
     return flat_ids * capacity + earlier
 
 
@@ -41,7 +373,7 @@
     expand_local = expand_weight[0]
     contract_local = contract_weight[0]
     full_width = contract_local.shape[1]
-    positions = slot_positions(expert_ids, capacity, experts)
+    positions = slot_positions(expert_ids, capacity)
     placement_matrix = (
         positions[:, None] == jnp.arange(slot_count, dtype=jnp.int32)[None, :]
     ).astype(jnp.bfloat16)
@@ -112,8 +444,9 @@
 
 
 def solution(mesh):
+    small = dict(mesh.shape) == {"sec": 2, "section": 4, "expert": 4}
     return jax.shard_map(
-        per_device,
+        fused if small else per_device,
         mesh=mesh,
         in_specs=(
             P("expert", ("sec", "section")),

time: 253 us -> 61.8 us (0.24)
  waiting for transfers between devices: 123 us -> 0 us
  blocking collectives: 70.4 us -> 0 us
  Pallas kernels: 0 us -> 52.8 us
  matrix products: 15.7 us -> 0 us
  between operations: 14.2 us -> 0.65 us
  starting transfers between devices: 13.2 us -> 0 us
  other arithmetic: 4.44 us -> 0 us
    psum x1 -> x0, waiting for transfers between devices: 76.7 us -> none  [per_device(): lax.psum(out_part, ('sec', 'section')).astype(jnp.float32)]
    pallas_call x0 -> x1, Pallas kernels: none -> 52.8 us  [fused(): pl.pallas_call(kernel, out_shape=(jax.ShapeDtypeStruct((tr, wd), BF16), j...]
    all_to_all x3 -> x0, waiting for transfers between devices: 46.2 us -> none  [the longest x1 17.6 us: per_device(): lax.all_to_all(back_rows, 'expert', split_axis=0, concat_axis=0, tiled=True)]
    all_gather x1 -> x0, blocking collectives: 30 us -> none  [per_device(): lax.all_gather(tokens, ('sec', 'section'), axis=1, tiled=True)]
    all_to_all x1 -> x0, blocking collectives: 24 us -> none  [per_device(): lax.all_to_all(out_rows, 'expert', split_axis=0, concat_axis=0, tiled=True)]
    psum x1 -> x0, blocking collectives: 16.4 us -> none  [per_device(): gate_grad = lax.psum(partial_dots, ('sec', 'section'))]
    dot_general x7 -> x0, matrix products: 15.7 us -> none  [the longest x1 5.43 us: transposed_product(): lax.dot_general(left, right, (((1,), (1,)), ((), ())), preferred_element_...]
    all_to_all x3 -> x0, starting transfers between devices: 13.1 us -> none  [the longest x1 4.47 us: per_device(): lax.all_to_all(back_rows, 'expert', split_axis=0, concat_axis=0, tiled=True)]
  transfers between devices with their start and end apart: 5 -> 0, of which waited for: 4 -> 0; matrix products, arithmetic and copies ran while one was open for 8% -> 0% of each run, Pallas kernels for 0% -> 0%
where the time goes in v1:
time: 61.8 us; the launch traced here: 61.5 us
  Pallas kernels  52.8 us (85%)
  local copies, waits for them, and re-layouts  8.03 us (13%)
  between operations  0.65 us (1%)
    pallas_call x1, Pallas kernels, fused(): pl.pallas_call(kernel, out_shape=(jax.ShapeDtypeStruct((tr, wd), BF16), j...  52.8 us
    unnamed x15, local copies, waits for them, and re-layouts  8.03 us

profile of v1, /device:TPU:0, one launch (start us, length us, event | category | flops | bytes accessed | tf_op | source)
XLA Modules:
  0.0 61.5 jit_solution(2132834690435086599)
XLA Ops:
  0.6 0.0 copy-start
  0.6 1.6 %copy-done = bf16[1,2048,512]{2,1,0:T(8,128)(2,1)S(1)} copy-done((bf16[1,2048,512]{2,1,0:T(8,128)(2,1)S(1)}, bf16[1,2048,512]{2,1,0:T(8,128)(2,1)}, u32[]{:S(2)}) %copy-start) | copy-done | bytes 2097176
  2.2 0.0 copy-start.1
  2.2 1.6 %copy-done.1 = bf16[1,512,2048]{2,1,0:T(8,128)(2,1)S(1)} copy-done((bf16[1,512,2048]{2,1,0:T(8,128)(2,1)S(1)}, bf16[1,512,2048]{2,1,0:T(8,128)(2,1)}, u32[]{:S(2)}) %copy-start.1) | copy-done | bytes 2097176
  3.8 0.0 copy-start.2
  3.8 0.8 %copy-done.2 = bf16[128,256]{1,0:T(8,128)(2,1)S(1)} copy-done((bf16[128,256]{1,0:T(8,128)(2,1)S(1)}, bf16[128,256]{1,0:T(8,128)(2,1)}, u32[]{:S(2)}) %copy-start.2) | copy-done | bytes 65560
  4.7 0.0 copy-start.3
  4.7 0.8 %copy-done.3 = bf16[128,256]{1,0:T(8,128)(2,1)S(1)} copy-done((bf16[128,256]{1,0:T(8,128)(2,1)S(1)}, bf16[128,256]{1,0:T(8,128)(2,1)}, u32[]{:S(2)}) %copy-start.3) | copy-done | bytes 65560
  5.5 0.0 copy-start.4
  5.5 0.7 %copy-done.4 = s32[128,2]{0,1:T(2,128)S(1)} copy-done((s32[128,2]{0,1:T(2,128)S(1)}, s32[128,2]{0,1:T(2,128)}, u32[]{:S(2)}) %copy-start.4) | copy-done | bytes 1048
  6.2 0.0 copy-start.5
  6.2 0.7 %copy-done.5 = f32[128,2]{0,1:T(2,128)S(1)} copy-done((f32[128,2]{0,1:T(2,128)S(1)}, f32[128,2]{0,1:T(2,128)}, u32[]{:S(2)}) %copy-start.5) | copy-done | bytes 1048
  6.9 52.8 %shard_map.85 = (bf16[128,256]{1,0:T(8,128)(2,1)S(1)}, bf16[128,256]{1,0:T(8,128)(2,1)S(1)}, f32[2,128]{1,0:T(2,128)S(1)}) custom-call(bf16[128,256]{1,0:T(8,128)(2,1)S(1)} %copy-done.2, bf16[128,256]{1,0:T(8,128)(2,1)S(1)} %copy-done.3, s32[2,128]{1,0:T(2,128)S(1)} %bitcast.4, f32[2,128]{1,0:T(2,128)S(1)} %bitcast.5, bf16[1,2048,512]{2,1,0:T(8,128)(2,1)S(1)} %copy-done, ...), custom_call_target="tpu_custom_call" | custom-call | flops 3221225472 | bytes 4194304 | tf_op jit(solution)/shard_map/pallas_call | solution.py:285
  59.7 0.6 %copy.12 = bf16[128,256]{1,0:T(8,128)(2,1)} copy(bf16[128,256]{1,0:T(8,128)(2,1)S(1)} %get-tuple-element.12) | data formatting | bytes 131072
  60.3 0.6 %copy.13 = bf16[128,256]{1,0:T(8,128)(2,1)} copy(bf16[128,256]{1,0:T(8,128)(2,1)S(1)} %get-tuple-element.13) | data formatting | bytes 131072
  60.9 0.6 copy.14
Async XLA Ops:
  0.6 1.6 %copy-start = (bf16[1,2048,512]{2,1,0:T(8,128)(2,1)S(1)}, bf16[1,2048,512]{2,1,0:T(8,128)(2,1)}, u32[]{:S(2)}) copy-start(bf16[1,2048,512]{2,1,0:T(8,128)(2,1)} %w1_hbm.1) | copy-start | bytes 6291460
  2.2 1.6 %copy-start.1 = (bf16[1,512,2048]{2,1,0:T(8,128)(2,1)S(1)}, bf16[1,512,2048]{2,1,0:T(8,128)(2,1)}, u32[]{:S(2)}) copy-start(bf16[1,512,2048]{2,1,0:T(8,128)(2,1)} %w2_hbm.1) | copy-start | bytes 6291460
  3.8 0.8 %copy-start.2 = (bf16[128,256]{1,0:T(8,128)(2,1)S(1)}, bf16[128,256]{1,0:T(8,128)(2,1)}, u32[]{:S(2)}) copy-start(bf16[128,256]{1,0:T(8,128)(2,1)} %tok.1) | copy-start | bytes 196612
  4.7 0.8 %copy-start.3 = (bf16[128,256]{1,0:T(8,128)(2,1)S(1)}, bf16[128,256]{1,0:T(8,128)(2,1)}, u32[]{:S(2)}) copy-start(bf16[128,256]{1,0:T(8,128)(2,1)} %cot.1) | copy-start | bytes 196612
  5.5 0.7 %copy-start.4 = (s32[128,2]{0,1:T(2,128)S(1)}, s32[128,2]{0,1:T(2,128)}, u32[]{:S(2)}) copy-start(s32[128,2]{0,1:T(2,128)} %param.8) | copy-start | bytes 3076
  6.2 0.7 %copy-start.5 = (f32[128,2]{0,1:T(2,128)S(1)}, f32[128,2]{0,1:T(2,128)}, u32[]{:S(2)}) copy-start(f32[128,2]{0,1:T(2,128)} %param.9) | copy-start | bytes 3076

commit v2 on v1

--- a/solution.py
+++ b/solution.py
@@ -32,6 +32,8 @@
     z = lax.axis_index("section")
     e = lax.axis_index("expert")
     zp = partners(z)
+    inner = (z * (3 - z)) // 2
+    zq = (z, zp[1], inner * zp[3] + (1 - inner) * zp[2], inner * zp[2] + (1 - inner) * zp[3])
     ep = partners(e)
 
     def to_z(s):
@@ -63,11 +65,22 @@
     pl.semaphore_wait(barrier, len(peers))
 
     sends = []
-    zc = {}
-    for s in (1, 2, 3):
-        zc[s] = rcopy(zbuf.at[0], zbuf.at[s], zsend.at[s], zrecv.at[s], to_z(s))
-        zc[s].start()
-        sends.append(zc[s])
+    zc = {
+        1: rcopy(zbuf.at[0], zbuf.at[1], zsend.at[1], zrecv.at[1], to_z(1)),
+        2: rcopy(zbuf.at[0], zbuf.at[2], zsend.at[2], zrecv.at[2], to_z(3)),
+        3: rcopy(zbuf.at[1], zbuf.at[3], zsend.at[3], zrecv.at[3], to_z(3)),
+        4: rcopy(zbuf.at[2], zbuf.at[2], zsend.at[4], zrecv.at[2], to_z(1)),
+        5: rcopy(zbuf.at[3], zbuf.at[3], zsend.at[5], zrecv.at[3], to_z(1)),
+    }
+    zc[1].start()
+    sends.append(zc[1])
+
+    def pass_on(i):
+        @pl.when(inner == 1)
+        def _():
+            zc[i].start()
+
+    pass_on(2)
 
     rid = lax.broadcasted_iota(jnp.int32, (8, tr), 0)
     erow = jnp.where(rid == 0, ep[0], jnp.where(rid == 1, ep[1], jnp.where(rid == 2, ep[2], jnp.where(rid == 3, ep[3], -1))))
@@ -89,17 +102,14 @@
         gslot[d] = jnp.broadcast_to(jnp.sum(weighed, axis=1, keepdims=True), (cap, wd))
         own[0, 0, d * cap : (d + 1) * cap, 0:tr] = one
         own[0, 1, d * cap : (d + 1) * cap, 0:tr] = weighed
-    pmat[...] = own[0, 0, :, 0:tr].T.astype(BF16)
-    pgate[...] = own[0, 1, :, 0:tr].T.astype(BF16)
-
-    cw1.wait()
-    cw2.wait()
-
-    def block(core, s):
-        return pl.ds(pl.multiple_of((core * 4 + zp[s]) * wd, wd), wd)
+    def block(core, zs):
+        return pl.ds(pl.multiple_of((core * 4 + zs) * wd, wd), wd)
 
     def gather_step(half, core, s, first):
-        at = block(core, s)
+        if first:
+            cw1.wait()
+            cw2.wait()
+        at = block(core, zq[s])
         xs = slots[half, s, :, 0].reshape(rows, wd)
         gs = slots[half, s, :, 1].reshape(rows, wd)
         hpart = jnp.dot(xs, w1[at, :], preferred_element_type=F32)
@@ -117,9 +127,10 @@
     def dispatch(s):
         if s:
             zc[s].wait_recv()
+            pass_on(s + 2)
         xb = zbuf[s, 0]
         cb = zbuf[s, 1]
-        for d in (3, 1, 2, 0):
+        for d in (1, 2, 3, 0):
             dst = slots.at[0, s, 0] if d == 0 else sendbuf.at[s, d]
             dst[0] = jnp.dot(pt[d], xb, preferred_element_type=F32).astype(BF16)
             dst[1] = (jnp.dot(pt[d], cb, preferred_element_type=F32) * gslot[d]).astype(BF16)
@@ -142,11 +153,13 @@
 
     dispatch(0)
     dispatch(1)
+    pmat[...] = own[0, 0, :, 0:tr].T.astype(BF16)
+    pgate[...] = own[0, 1, :, 0:tr].T.astype(BF16)
+    dispatch(2)
+    dispatch(3)
     take(0)
-    dispatch(2)
     take(1)
     take_sib(0)
-    dispatch(3)
     take(2)
     take_sib(1)
     take(3)
@@ -157,7 +170,7 @@
     cubic = 0.044715
     lane = lax.broadcasted_iota(jnp.int32, (cap, 128), 1)
     xc = {}
-    for d in (3, 1, 2, 0):
+    for d in (1, 2, 3, 0):
         rr = slice(d * cap, (d + 1) * cap)
         h = hid[rr, :]
         ga = gact[rr, :]
@@ -185,7 +198,7 @@
 
     def expand_back(s):
         for core, mine in ((1 - c, False), (c, True)):
-            at = block(core, s)
+            at = block(core, zp[s])
             o = jnp.dot(act[...], w2[:, at], preferred_element_type=F32)
             b = lax.dot_general(ghid[...], w1[at, :], (((1,), (1,)), ((), ())), preferred_element_type=F32)
             if mine:
@@ -200,7 +213,7 @@
 
     def give_back(s):
         bc[s].wait_recv()
-        for d in (3, 1, 2, 0):
+        for d in (1, 2, 3, 0):
             rr = slice(d * cap, (d + 1) * cap)
             dst = ret.at[s, 0] if d == 0 else rsend.at[s, d]
             for k in range(2):
@@ -273,6 +286,11 @@
     for d in sends:
         d.wait_send()
 
+    @pl.when(inner == 1)
+    def _():
+        for i in (2, 3, 4, 5):
+            zc[i].wait_send()
+
 
 def fused(tokens, cotangent, expert_ids, gate_values, expand_weight, contract_weight):
     tr, wd = tokens.shape
@@ -280,7 +298,7 @@
     width, ff = expand_weight.shape[1:]
     rows = 4 * cap
     vm = pl.BlockSpec(memory_space=pltpu.VMEM)
-    anyspace = pl.BlockSpec(memory_space=pl.ANY)
+    anyspace = pl.BlockSpec(memory_space=pltpu.HBM)
     dma = pltpu.SemaphoreType.DMA
     comb, grad, gg = pl.pallas_call(
         kernel,
@@ -317,7 +335,7 @@
             pltpu.VMEM((4, 2, tr, wd), BF16),
             pltpu.VMEM((2, tr, wd), F32),
             dma((2,)),
-            dma((4,)), dma((4,)),
+            dma((6,)), dma((4,)),
             dma((4, 4)), dma((4, 4)),
             dma((4,)), dma((4,)),
             dma((4,)), dma((4,)),

time: 61.8 us -> 60.4 us (0.977)
  Pallas kernels: 52.8 us -> 51.4 us
    pallas_call x1, Pallas kernels: 52.8 us -> 51.4 us  [fused(): pl.pallas_call(kernel, out_shape=(jax.ShapeDtypeStruct((tr, wd), BF16), j...]
where the time goes in v2:
time: 60.4 us; the launch traced here: 60.1 us
  Pallas kernels  51.4 us (85%)
  local copies, waits for them, and re-layouts  8.03 us (13%)
  between operations  0.65 us (1%)
    pallas_call x1, Pallas kernels, fused(): pl.pallas_call(kernel, out_shape=(jax.ShapeDtypeStruct((tr, wd), BF16), j...  51.4 us
    unnamed x15, local copies, waits for them, and re-layouts  8.03 us

profile of v2, /device:TPU:0, one launch (start us, length us, event | category | flops | bytes accessed | tf_op | source)
XLA Modules:
  0.0 60.1 jit_solution(1500795756891018361)
XLA Ops:
  0.6 0.0 copy-start
  0.6 1.6 %copy-done = bf16[1,2048,512]{2,1,0:T(8,128)(2,1)S(1)} copy-done((bf16[1,2048,512]{2,1,0:T(8,128)(2,1)S(1)}, bf16[1,2048,512]{2,1,0:T(8,128)(2,1)}, u32[]{:S(2)}) %copy-start) | copy-done | bytes 2097176
  2.2 0.0 copy-start.1
  2.2 1.6 %copy-done.1 = bf16[1,512,2048]{2,1,0:T(8,128)(2,1)S(1)} copy-done((bf16[1,512,2048]{2,1,0:T(8,128)(2,1)S(1)}, bf16[1,512,2048]{2,1,0:T(8,128)(2,1)}, u32[]{:S(2)}) %copy-start.1) | copy-done | bytes 2097176
  3.8 0.0 copy-start.2
  3.8 0.8 %copy-done.2 = bf16[128,256]{1,0:T(8,128)(2,1)S(1)} copy-done((bf16[128,256]{1,0:T(8,128)(2,1)S(1)}, bf16[128,256]{1,0:T(8,128)(2,1)}, u32[]{:S(2)}) %copy-start.2) | copy-done | bytes 65560
  4.7 0.0 copy-start.3
  4.7 0.8 %copy-done.3 = bf16[128,256]{1,0:T(8,128)(2,1)S(1)} copy-done((bf16[128,256]{1,0:T(8,128)(2,1)S(1)}, bf16[128,256]{1,0:T(8,128)(2,1)}, u32[]{:S(2)}) %copy-start.3) | copy-done | bytes 65560
  5.5 0.0 copy-start.4
  5.5 0.7 %copy-done.4 = s32[128,2]{0,1:T(2,128)S(1)} copy-done((s32[128,2]{0,1:T(2,128)S(1)}, s32[128,2]{0,1:T(2,128)}, u32[]{:S(2)}) %copy-start.4) | copy-done | bytes 1048
  6.2 0.0 copy-start.5
  6.2 0.7 %copy-done.5 = f32[128,2]{0,1:T(2,128)S(1)} copy-done((f32[128,2]{0,1:T(2,128)S(1)}, f32[128,2]{0,1:T(2,128)}, u32[]{:S(2)}) %copy-start.5) | copy-done | bytes 1048
  6.9 51.4 %shard_map.85 = (bf16[128,256]{1,0:T(8,128)(2,1)S(1)}, bf16[128,256]{1,0:T(8,128)(2,1)S(1)}, f32[2,128]{1,0:T(2,128)S(1)}) custom-call(bf16[128,256]{1,0:T(8,128)(2,1)S(1)} %copy-done.2, bf16[128,256]{1,0:T(8,128)(2,1)S(1)} %copy-done.3, s32[2,128]{1,0:T(2,128)S(1)} %bitcast.4, f32[2,128]{1,0:T(2,128)S(1)} %bitcast.5, bf16[1,2048,512]{2,1,0:T(8,128)(2,1)S(1)} %copy-done, ...), custom_call_target="tpu_custom_call" | custom-call | flops 3221225472 | bytes 4194304 | tf_op jit(solution)/shard_map/pallas_call | solution.py:303
  58.3 0.6 %copy.12 = bf16[128,256]{1,0:T(8,128)(2,1)} copy(bf16[128,256]{1,0:T(8,128)(2,1)S(1)} %get-tuple-element.12) | data formatting | bytes 131072
  58.9 0.6 %copy.13 = bf16[128,256]{1,0:T(8,128)(2,1)} copy(bf16[128,256]{1,0:T(8,128)(2,1)S(1)} %get-tuple-element.13) | data formatting | bytes 131072
  59.6 0.6 copy.14
Async XLA Ops:
  0.6 1.6 %copy-start = (bf16[1,2048,512]{2,1,0:T(8,128)(2,1)S(1)}, bf16[1,2048,512]{2,1,0:T(8,128)(2,1)}, u32[]{:S(2)}) copy-start(bf16[1,2048,512]{2,1,0:T(8,128)(2,1)} %w1_hbm.1) | copy-start | bytes 6291460
  2.2 1.6 %copy-start.1 = (bf16[1,512,2048]{2,1,0:T(8,128)(2,1)S(1)}, bf16[1,512,2048]{2,1,0:T(8,128)(2,1)}, u32[]{:S(2)}) copy-start(bf16[1,512,2048]{2,1,0:T(8,128)(2,1)} %w2_hbm.1) | copy-start | bytes 6291460
  3.8 0.8 %copy-start.2 = (bf16[128,256]{1,0:T(8,128)(2,1)S(1)}, bf16[128,256]{1,0:T(8,128)(2,1)}, u32[]{:S(2)}) copy-start(bf16[128,256]{1,0:T(8,128)(2,1)} %tok.1) | copy-start | bytes 196612
  4.7 0.8 %copy-start.3 = (bf16[128,256]{1,0:T(8,128)(2,1)S(1)}, bf16[128,256]{1,0:T(8,128)(2,1)}, u32[]{:S(2)}) copy-start(bf16[128,256]{1,0:T(8,128)(2,1)} %cot.1) | copy-start | bytes 196612
  5.5 0.7 %copy-start.4 = (s32[128,2]{0,1:T(2,128)S(1)}, s32[128,2]{0,1:T(2,128)}, u32[]{:S(2)}) copy-start(s32[128,2]{0,1:T(2,128)} %param.8) | copy-start | bytes 3076
  6.2 0.7 %copy-start.5 = (f32[128,2]{0,1:T(2,128)S(1)}, f32[128,2]{0,1:T(2,128)}, u32[]{:S(2)}) copy-start(f32[128,2]{0,1:T(2,128)} %param.9) | copy-start | bytes 3076
